TPU v7x, 256 devices: a whole 4x4x8 slice. The times are simulated.
256 devices in a mesh: row: 16 (over x_hi, y, core), col: 16 (over x_lo, z).
Axes of the slice: x: 4 (x_hi: 2, x_lo: 2; x = x_hi * 2 + x_lo), y: 4, z: 8, core: 2. Of those that a mesh axis runs over, the one named last changes fastest.
Arguments:
- pair_map: bfloat16 [512, 512, 128], P('row', 'col'), may hold values from -6 to 6
- token_mask: int32 [512], replicated, may hold values 0 or 1
- norm_gain: float32 [2, 128], replicated, may hold values from 0.1 to 1.9
- norm_bias: float32 [2, 128], replicated, may hold values from -3 to 3
- proj_weight: bfloat16 [2, 128, 256], replicated, may hold values from -0.5 to 0.5
- gate_weight: bfloat16 [2, 128, 256], replicated, may hold values from -0.5 to 0.5
- out_gain: float32 [2, 128], replicated, may hold values from 0.1 to 1.9
- out_bias: float32 [2, 128], replicated, may hold values from -3 to 3
- final_weight: bfloat16 [2, 128, 128], replicated, may hold values from -0.5 to 0.5
- output_gate: bfloat16 [2, 128, 128], replicated, may hold values from -0.5 to 0.5
Outputs:
- updated_pair: bfloat16 [512, 512, 128], P('row', 'col')
Inputs may be any that keep to these rules, and one draw needn't show every extreme that they name: `token_mask`: 1 marks a real token, 0 a padding token.
All inputs are finite; a program needn't handle non-finite values.
Results may differ from a plain program's by a relative error of at most 0.014.
Values may be sent and summed in bfloat16 or wider, within the bound.
A program may use at most 128 MiB of HBM per device.

v0:
```python
import jax
import jax.numpy as jnp
from jax import lax
from jax.sharding import PartitionSpec as P


def normalize(values, gain_vector, bias_vector):
    average = jnp.mean(values, axis=-1, keepdims=True)
    centred = values - average
    variance = jnp.mean(centred * centred, axis=-1, keepdims=True)
    return centred * lax.rsqrt(variance + 1e-05) * gain_vector + bias_vector


def project(
    pair_map, pair_mask, norm_gain, norm_bias, proj_weight, gate_weight, output_gate, layer_id
):
    normed = normalize(
        pair_map.astype(jnp.float32), norm_gain[layer_id], norm_bias[layer_id]
    ).astype(jnp.bfloat16)
    projected = jnp.dot(normed, proj_weight[layer_id], preferred_element_type=jnp.float32)
    gating = jnp.dot(normed, gate_weight[layer_id], preferred_element_type=jnp.float32)
    halves = (jax.nn.sigmoid(gating) * projected * pair_mask[..., None]).astype(jnp.bfloat16)
    closing = jax.nn.sigmoid(
        jnp.dot(normed, output_gate[layer_id], preferred_element_type=jnp.float32)
    )
    return (halves, closing)


def finish(pair_map, summed, closing, out_gain, out_bias, final_weight, layer_id):
    lifted = normalize(summed.astype(jnp.float32), out_gain[layer_id], out_bias[layer_id]).astype(
        jnp.bfloat16
    )
    update = closing * jnp.dot(lifted, final_weight[layer_id], preferred_element_type=jnp.float32)
    return (pair_map.astype(jnp.float32) + update).astype(jnp.bfloat16)


def shards(
    pair_map,
    token_mask,
    norm_gain,
    norm_bias,
    proj_weight,
    gate_weight,
    out_gain,
    out_bias,
    final_weight,
    output_gate,
):
    rows_here = pair_map.shape[0]
    cols_here = pair_map.shape[1]
    hidden = proj_weight.shape[2] // 2
    row_mask = lax.dynamic_slice_in_dim(
        token_mask, lax.axis_index("row") * rows_here, rows_here
    ).astype(jnp.float32)
    col_mask = lax.dynamic_slice_in_dim(
        token_mask, lax.axis_index("col") * cols_here, cols_here
    ).astype(jnp.float32)
    pair_mask = row_mask[:, None] * col_mask[None, :]
    halves, closing = project(
        pair_map, pair_mask, norm_gain, norm_bias, proj_weight, gate_weight, output_gate, 0
    )
    left_side = halves[..., :hidden]
    right_side = halves[..., hidden:]
    right_rows = lax.all_gather(right_side, "row", axis=0, tiled=True)
    partial_value = jnp.einsum(
        "ikh,jkh->ijh", left_side, right_rows, preferred_element_type=jnp.float32
    )
    summed = lax.psum_scatter(partial_value, "col", scatter_dimension=1, tiled=True).astype(
        jnp.bfloat16
    )
    pair_map = finish(pair_map, summed, closing, out_gain, out_bias, final_weight, 0)
    halves, closing = project(
        pair_map, pair_mask, norm_gain, norm_bias, proj_weight, gate_weight, output_gate, 1
    )
    left_side = halves[..., :hidden]
    right_side = halves[..., hidden:]
    left_cols = lax.all_gather(left_side, "col", axis=1, tiled=True)
    partial_value = jnp.einsum(
        "kih,kjh->ijh", left_cols, right_side, preferred_element_type=jnp.float32
    )
    summed = lax.psum_scatter(partial_value, "row", scatter_dimension=0, tiled=True).astype(
        jnp.bfloat16
    )
    return finish(pair_map, summed, closing, out_gain, out_bias, final_weight, 1)


def solution(mesh):
    return jax.shard_map(
        shards,
        mesh=mesh,
        in_specs=(P("row", "col", None), P(), P(), P(), P(), P(), P(), P(), P(), P()),
        out_specs=P("row", "col", None),
        check_vma=False,
    )
```

profile of v0, /device:TPU:1, one launch (start us, length us, event | category | flops | bytes accessed | tf_op | source)
XLA Modules:
  0.0 448.8 jit_solution(17538619337422286190)
XLA Ops:
  6.5 1.2 convert_reduce_fusion
  7.7 1.3 fusion.29
  9.0 0.8 slice_bitcast_fusion.2
  9.8 0.8 dynamic-slice_convert_fusion.1
  10.7 1.4 fusion.50
  12.1 1.4 fusion.11
  13.6 0.8 fusion.70
  14.5 1.4 copy.48
  15.9 63.2 %all-gather.3.cloned.1.call-done = bf16[512,32,128]{2,1,0:T(8,128)(2,1)} async-done(((bf16[32,32,128]{2,1,0:T(8,128)(2,1)}), bf16[512,32,128]{2,1,0:T(8,128)(2,1)}) %all-gather.3.cloned.1.call-update) | async-done | bytes 4194320 | tf_op jit(solution)/shard_map/all_gather | solution.py:64
  79.1 23.0 %copy.47 = bf16[512,32,128]{1,0,2:T(8,128)(2,1)} copy(bf16[512,32,128]{2,1,0:T(8,128)(2,1)} %all-gather.3.cloned.1.call-done) | data formatting | bytes 8388608 | tf_op jit(solution)/shard_map/all_gather | solution.py:64
  102.1 11.3 %convolution_bitcast_fusion.1 = f32[32,512,128]{1,0,2:T(8,128)} fusion(bf16[512,32,128]{1,0,2:T(8,128)(2,1)} %copy.47, bf16[32,32,128]{1,0,2:T(8,128)(2,1)S(1)} %copy.48), kind=kOutput, calls=%fused_computation.1 | convolution fusion | flops 134217728 | bytes 12845056 | tf_op jit(solution)/shard_map/ikh,jkh->ijh/dot_general | solution.py:65
  113.4 11.0 %copy.49 = f32[32,512,128]{2,0,1:T(8,128)} copy(f32[32,512,128]{1,0,2:T(8,128)} %convolution_bitcast_fusion.1) | data formatting | bytes 16777216 | tf_op jit(solution)/shard_map/ikh,jkh->ijh/transpose | solution.py:65
  124.5 0.6 copy-done.3
  125.4 0.5 fusion.17
  125.9 97.4 %reduce-scatter.3.cloned.1.call-done = f32[32,32,128]{2,0,1:T(8,128)} async-done(((f32[32,512,128]{2,0,1:T(8,128)}), f32[32,32,128]{2,0,1:T(8,128)}) %reduce-scatter.3.cloned.1.call-update) | async-done | bytes 524304 | tf_op jit(solution)/shard_map/reduce_scatter | solution.py:68
  223.3 1.2 convert_reduce_fusion.2
  224.7 1.4 fusion.37
  226.3 1.4 fusion.40
  227.7 0.4 fusion.71
  228.1 0.4 multiply_reduce_fusion
  228.5 0.3 add_convert_fusion
  229.2 0.4 fusion.10
  229.6 0.8 fusion.69
  230.7 1.6 copy.55
  232.3 64.1 %all-gather.5.cloned.1.call-done = bf16[32,512,128]{2,1,0:T(8,128)(2,1)} async-done(((bf16[32,32,128]{2,1,0:T(8,128)(2,1)}), bf16[32,512,128]{2,1,0:T(8,128)(2,1)}) %all-gather.5.cloned.1.call-update) | async-done | bytes 4194320 | tf_op jit(solution)/shard_map/all_gather | solution.py:77
  296.3 7.9 %copy.56 = bf16[32,512,128]{1,0,2:T(8,128)(2,1)} copy(bf16[32,512,128]{2,1,0:T(8,128)(2,1)} %all-gather.5.cloned.1.call-done) | data formatting | bytes 8388608 | tf_op jit(solution)/shard_map/all_gather | solution.py:77
  304.2 6.6 %convolution_bitcast_fusion = f32[512,32,128]{0,1,2:T(8,128)} fusion(bf16[32,32,128]{0,1,2:T(8,128)(2,1)S(1)} %copy.55, bf16[32,512,128]{1,0,2:T(8,128)(2,1)} %copy.56), kind=kOutput, calls=%fused_computation | convolution fusion | flops 134217728 | bytes 12845056 | tf_op jit(solution)/shard_map/kih,kjh->ijh/dot_general | solution.py:78
  310.9 10.9 %copy.57 = f32[512,32,128]{2,1,0:T(8,128)} copy(f32[512,32,128]{0,1,2:T(8,128)} %convolution_bitcast_fusion) | data formatting | bytes 16777216 | tf_op jit(solution)/shard_map/kih,kjh->ijh/transpose | solution.py:78
  322.1 115.3 %reduce-scatter.5.cloned.1.call-done = f32[32,32,128]{2,1,0:T(8,128)} async-done(((f32[512,32,128]{2,1,0:T(8,128)}), f32[32,32,128]{2,1,0:T(8,128)}) %reduce-scatter.5.cloned.1.call-update) | async-done | bytes 524304 | tf_op jit(solution)/shard_map/reduce_scatter | solution.py:81
  437.4 1.2 convert_reduce_fusion.1
  438.7 1.4 fusion.33
  440.1 2.2 fusion.20
  (36 shorter events, 1.7 us)
Async XLA Ops:
  6.5 72.6 %all-gather.3.cloned.1.call-start = ((), (), s32[]{:S(2)}) async-start(), calls=%async_computation.2 | async-start | bytes 4456448 | tf_op jit(solution)/shard_map/all_gather | solution.py:64
  14.4 208.9 %reduce-scatter.3.cloned.1.call-start = ((), (), s32[]{:S(2)}) async-start(), calls=%async_computation.3 | async-start | bytes 8912896 | tf_op jit(solution)/shard_map/reduce_scatter | solution.py:68
  124.4 0.7 copy-start.3
  124.4 0.7 copy-start.4
  124.4 1.0 copy-start
  124.4 1.0 copy-start.6
  124.4 103.3 %copy-start.2 = (bf16[2,128,128]{2,1,0:T(8,128)(2,1)S(1)}, bf16[2,128,128]{2,1,0:T(8,128)(2,1)}, u32[]{:S(2)}) copy-start(bf16[2,128,128]{2,1,0:T(8,128)(2,1)} %param.18) | copy-start | bytes 196612
  124.4 104.4 %copy-start.1 = (bf16[2,128,256]{2,1,0:T(8,128)(2,1)S(1)}, bf16[2,128,256]{2,1,0:T(8,128)(2,1)}, u32[]{:S(2)}) copy-start(bf16[2,128,256]{2,1,0:T(8,128)(2,1)} %param.14) | copy-start | bytes 393220
  124.5 104.7 %copy-start.5 = (bf16[2,128,256]{2,1,0:T(8,128)(2,1)S(1)}, bf16[2,128,256]{2,1,0:T(8,128)(2,1)}, u32[]{:S(2)}) copy-start(bf16[2,128,256]{2,1,0:T(8,128)(2,1)} %param.15) | copy-start | bytes 393220
  124.5 171.8 %all-gather.5.cloned.1.call-start = ((), (), s32[]{:S(2)}) async-start(), calls=%async_computation.4 | async-start | bytes 4456448 | tf_op jit(solution)/shard_map/all_gather | solution.py:77
  230.4 207.0 %reduce-scatter.5.cloned.1.call-start = ((), (), s32[]{:S(2)}) async-start(), calls=%async_computation.5 | async-start | bytes 8912896 | tf_op jit(solution)/shard_map/reduce_scatter | solution.py:81
Sparse Core Ops, SparseCore 0:
  14.5 64.5 all-gather.2
  124.6 98.6 reduce-scatter.2
  230.5 65.7 all-gather.4
  321.9 115.3 reduce-scatter.4
where the time goes:
time: 450 us; the launch traced here: 449 us
  waiting for transfers between devices  340 us (76%)
  local copies, waits for them, and re-layouts  59.4 us (13%)
  matrix products  24.9 us (6%)
  between operations  13.3 us (3%)
  other arithmetic  10.9 us (2%)
    reduce_scatter x1, waiting for transfers between devices, shards(): lax.psum_scatter(partial_value, 'row', scatter_dimension=0, tiled=True)  115 us
    reduce_scatter x1, waiting for transfers between devices, shards(): lax.psum_scatter(partial_value, 'col', scatter_dimension=1, tiled=True)  97.4 us
    all_gather x1, waiting for transfers between devices, shards(): left_cols = lax.all_gather(left_side, 'col', axis=1, tiled=True)  64.1 us
    all_gather x1, waiting for transfers between devices, shards(): right_rows = lax.all_gather(right_side, 'row', axis=0, tiled=True)  63.2 us
    all_gather x1, local copies, waits for them, and re-layouts, shards(): right_rows = lax.all_gather(right_side, 'row', axis=0, tiled=True)  23 us
    dot_general x1, matrix products, shards(): jnp.einsum('ikh,jkh->ijh', left_side, right_rows, preferred_element_type=...  11.3 us
    transpose x1, local copies, waits for them, and re-layouts, shards(): jnp.einsum('ikh,jkh->ijh', left_side, right_rows, preferred_element_type=...  11 us
    transpose x1, local copies, waits for them, and re-layouts, shards(): jnp.einsum('kih,kjh->ijh', left_cols, right_side, preferred_element_type=...  10.9 us
  transfers between devices with their start and end apart: 4, of which 4 were waited for; matrix products, arithmetic and copies ran while one was open for 1% of the time, Pallas kernels for 0%

commit v1 on v0

v1 whole, which is shorter than its diff:
```python
import jax
import jax.numpy as jnp
from jax import lax
from jax.experimental import pallas as pl
from jax.experimental.pallas import tpu as pltpu
from jax.sharding import PartitionSpec as P

MESH = pl.DeviceIdType.MESH
F32 = jnp.float32
BF16 = jnp.bfloat16


def place():
    r = lax.axis_index("row")
    c = lax.axis_index("col")
    return r // 8, (r // 2) % 4, r % 2, c // 8, c % 8


def partner(me, n):
    x_hi, y, core, x_lo, z = me
    x2 = (x_hi * 2 + x_lo + n // 32) % 4
    y2 = (y + (n // 8) % 4) % 4
    z2 = (z + n % 8) % 8
    rr = (x2 // 2) * 4 + y2
    col = (x2 % 2) * 8 + z2
    return rr * 2 + core, col, rr * 16 + col


def dot(a, b, dims):
    return lax.dot_general(a, b, (dims, ((), ())), preferred_element_type=F32)


def sigmoid(v):
    return 0.5 * jnp.tanh(0.5 * v) + 0.5


def normalize(v, gain, bias):
    average = jnp.mean(v, axis=0, keepdims=True)
    centred = v - average
    variance = jnp.mean(centred * centred, axis=0, keepdims=True)
    return centred * lax.rsqrt(variance + 1e-05) * gain + bias


def chunk_swap(v):
    lane = lax.broadcasted_iota(jnp.int32, v[0].shape, 1)
    odd = (lane // 32) % 2 == 1
    high = lane >= 64

    def pair(a, b, shift, mask):
        return jnp.where(mask, pltpu.roll(b, shift, 1), a), jnp.where(
            mask, b, pltpu.roll(a, 128 - shift, 1)
        )

    a, b = pair(v[0], v[1], 32, odd)
    c, d = pair(v[2], v[3], 32, odd)
    a, c = pair(a, c, 64, high)
    b, d = pair(b, d, 64, high)
    return a, b, c, d


def kernel(
    x_ref, mask_ref, ng_ref, nb_ref, pw_ref, gw_ref, og_ref, ob_ref, fw_ref, ow_ref,
    out_ref,
    wt, ft, gb, zt, close, half, fsend, frecv, left, right, left_in, right_in, sums, bsend, brecv, wide,
    entry, f_send, f_recv, b_send, b_recv, x_send, x_recv,
):
    me = place()
    x_hi, y, core, x_lo, z = me
    row, col = lax.axis_index("row"), lax.axis_index("col")
    chip = (x_hi * 4 + y) * 16 + x_lo * 8 + z
    other = (row + 1 - 2 * core, col)

    barrier = pltpu.get_barrier_semaphore()
    ys = [partner(me, 8 * d)[:2] for d in range(1, 4)]
    xs = [partner(me, 32 * d)[:2] for d in range(1, 4)]
    zs = [partner(me, d)[:2] for d in range(1, 8)]
    for device in [other] + zs + ys + xs:
        pl.semaphore_signal(barrier, inc=1, device_id=device, device_id_type=MESH)

    lane = lax.broadcasted_iota(jnp.int32, (8, 128), 1)
    first = lax.broadcasted_iota(jnp.int32, (8, 128), 0) + 8 * (lane // 32)
    row_mask = jnp.zeros((8, 128), jnp.int32)
    col_mask = jnp.zeros((8, 128), jnp.int32)
    for a in range(32):
        row_mask = jnp.where(first == a, mask_ref[row * 32 + a], row_mask)
        col_mask = jnp.where(lane % 32 == a, mask_ref[col * 32 + a], col_mask)
    token_mask = row_mask.astype(F32) * col_mask.astype(F32)
    for u in range(2):
        for k in range(2):
            wt[u, pl.ds(128 * k, 128)] = pw_ref[u, :, pl.ds(128 * k, 128)].T
            wt[u, pl.ds(256 + 128 * k, 128)] = gw_ref[u, :, pl.ds(128 * k, 128)].T
        wt[u, pl.ds(512, 128)] = ow_ref[u].T
        ft[u] = fw_ref[u].T
        for k, ref in enumerate((ng_ref, nb_ref, og_ref, ob_ref)):
            gb[4 * u + k] = jnp.broadcast_to(ref[pl.ds(u, 1), :], (128, 128)).T

    def project(u, s, z_s):
        normed = normalize(z_s, gb[4 * u], gb[4 * u + 1]).astype(BF16)
        product = dot(wt[u], normed, ((1,), (0,)))
        close[s] = sigmoid(product[512:])
        half[pl.ds(s, 256, stride=8), :] = (
            sigmoid(product[256:512]) * product[:256] * token_mask[s : s + 1]
        )

    def send_halves(u):
        @pl.loop(0, 128)
        def _(n):
            to_row, to_col, p = partner(me, n)
            rows = pl.multiple_of(p * 8, 8)
            fsend[u, p] = jnp.concatenate(
                [half[pl.ds(rows, 8), :], half[pl.ds(rows + 1024, 8), :]], axis=0
            ).astype(BF16)

            @pl.when(n > 0)
            def _():
                pltpu.make_async_remote_copy(
                    fsend.at[u, p], frecv.at[u, chip], f_send.at[u], f_recv.at[u],
                    device_id=(to_row, to_col), device_id_type=MESH,
                ).start()

        pltpu.make_async_copy(fsend.at[u, chip], frecv.at[u, chip], f_recv.at[u]).start()

    def whole(src, dst, send, recv):
        return pltpu.make_async_remote_copy(
            src, dst, send, recv, device_id=other, device_id_type=MESH
        )

    def arrange(u):
        whole(fsend.at[u], frecv.at[u], f_send.at[u], f_recv.at[u]).wait_recv()

        @pl.loop(0, 8)
        def _(rr):
            for t in range(2):
                for g in range(2):
                    tiles = [
                        frecv[u, rr * 16 + 2 * (4 * g + k) + t].astype(F32) for k in range(4)
                    ]
                    swapped = chunk_swap(tiles)
                    rows = pl.ds(pl.multiple_of(rr * 32, 32), 32)
                    lanes = pl.ds(128 * g, 128)
                    left[u, t, rows, lanes] = jnp.concatenate(
                        [v[:8] for v in swapped], axis=0
                    ).astype(BF16)
                    right[u, t, rows, lanes] = jnp.concatenate(
                        [v[8:] for v in swapped], axis=0
                    ).astype(BF16)

    def send_sums(u):
        @pl.loop(0, 8)
        def _(rr):
            for t in range(2):
                for g in range(2):
                    tiles = [
                        sums[t, pl.ds(pl.multiple_of(rr * 32, 32) + 8 * k, 8), pl.ds(128 * g, 128)]
                        for k in range(4)
                    ]
                    for k, tile in enumerate(chunk_swap(tiles)):
                        bsend[u, rr * 16 + 2 * (4 * g + k) + t] = tile.astype(BF16)

        @pl.loop(1, 128)
        def _(n):
            to_row, to_col, p = partner(me, n)
            pltpu.make_async_remote_copy(
                bsend.at[u, p], brecv.at[u, chip], b_send.at[u], b_recv.at[u],
                device_id=(to_row, to_col), device_id_type=MESH,
            ).start()

        pltpu.make_async_copy(bsend.at[u, chip], brecv.at[u, chip], b_recv.at[u]).start()
        whole(bsend.at[u], brecv.at[u], b_send.at[u], b_recv.at[u]).wait_recv()
        wide[...] = brecv[u].astype(F32).reshape(1024, 128)

    def finish(u, s):
        summed = wide[pl.ds(s, 128, stride=8), :]
        lifted = normalize(summed, gb[4 * u + 2], gb[4 * u + 3]).astype(BF16)
        update = close[s] * dot(ft[u], lifted, ((1,), (0,)))
        return (zt[s].astype(F32) + update).astype(BF16)

    for s in range(8):
        z_s = jnp.concatenate([x_ref[8 * k + s] for k in range(4)], axis=0).T
        zt[s] = z_s
        project(0, s, z_s.astype(F32))

    pl.semaphore_wait(barrier, 14)
    for device in ys:
        pl.semaphore_signal(entry.at[0], inc=1, device_id=device, device_id_type=MESH)
    pl.semaphore_wait(entry.at[0], 3)
    for device in xs:
        pl.semaphore_signal(entry.at[1], inc=1, device_id=device, device_id_type=MESH)
    pl.semaphore_wait(entry.at[1], 3)

    send_halves(0)
    arrange(0)
    swap = whole(right.at[0], right_in.at[0], x_send.at[0], x_recv.at[0])
    swap.start()

    def outgoing(t, operand):
        sums[t] = dot(left[0, 0], operand[0], ((1,), (1,))) + dot(
            left[0, 1], operand[1], ((1,), (1,))
        )

    outgoing(core, right.at[0])
    swap.wait_recv()
    outgoing(1 - core, right_in.at[0])
    send_sums(0)

    for s in range(8):
        z_s = finish(0, s)
        zt[s] = z_s
        project(1, s, z_s.astype(F32))

    send_halves(1)
    arrange(1)
    swap_left = whole(left.at[1, 1 - core], left_in, x_send.at[1], x_recv.at[1])
    swap_right = whole(right.at[1], right_in.at[1], x_send.at[2], x_recv.at[2])
    swap_left.start()
    swap_right.start()
    for t in range(2):
        sums[t] = dot(left[1, core], right[1, t], ((0,), (0,)))
    swap_left.wait_recv()
    swap_right.wait_recv()
    for t in range(2):
        sums[t] = sums[t] + dot(left_in[...], right_in[1, t], ((0,), (0,)))
    send_sums(1)

    for s in range(8):
        z_s = finish(1, s).T
        for k in range(4):
            out_ref[8 * k + s] = z_s[32 * k : 32 * k + 32]

    swap.wait_send()
    swap_left.wait_send()
    swap_right.wait_send()
    most = pl.ds(0, 127)
    for u in range(2):
        whole(fsend.at[u, most], frecv.at[u, most], f_send.at[u], f_recv.at[u]).wait_send()
        whole(bsend.at[u, most], brecv.at[u, most], b_send.at[u], b_recv.at[u]).wait_send()


def shards(*arrays):
    vmem = pl.BlockSpec(memory_space=pltpu.VMEM)
    smem = pl.BlockSpec(memory_space=pltpu.SMEM)
    return pl.pallas_call(
        kernel,
        out_shape=jax.ShapeDtypeStruct(arrays[0].shape, BF16),
        in_specs=[vmem, smem] + [vmem] * 8,
        out_specs=vmem,
        scratch_shapes=[
            pltpu.VMEM((2, 640, 128), BF16),
            pltpu.VMEM((2, 128, 128), BF16),
            pltpu.VMEM((8, 128, 128), F32),
            pltpu.VMEM((8, 128, 128), BF16),
            pltpu.VMEM((8, 128, 128), F32),
            pltpu.VMEM((2048, 128), F32),
            pltpu.VMEM((2, 128, 16, 128), BF16),
            pltpu.VMEM((2, 128, 16, 128), BF16),
            pltpu.VMEM((2, 2, 256, 256), BF16),
            pltpu.VMEM((2, 2, 256, 256), BF16),
            pltpu.VMEM((256, 256), BF16),
            pltpu.VMEM((2, 2, 256, 256), BF16),
            pltpu.VMEM((2, 256, 256), F32),
            pltpu.VMEM((2, 128, 8, 128), BF16),
            pltpu.VMEM((2, 128, 8, 128), BF16),
            pltpu.VMEM((1024, 128), F32),
            pltpu.SemaphoreType.REGULAR((2,)),
            pltpu.SemaphoreType.DMA((2,)),
            pltpu.SemaphoreType.DMA((2,)),
            pltpu.SemaphoreType.DMA((2,)),
            pltpu.SemaphoreType.DMA((2,)),
            pltpu.SemaphoreType.DMA((3,)),
            pltpu.SemaphoreType.DMA((3,)),
        ],
        compiler_params=pltpu.CompilerParams(
            collective_id=0, has_side_effects=True, vmem_limit_bytes=32 << 20
        ),
    )(*arrays)


def solution(mesh):
    return jax.shard_map(
        shards,
        mesh=mesh,
        in_specs=(P("row", "col", None), P(), P(), P(), P(), P(), P(), P(), P(), P()),
        out_specs=P("row", "col", None),
        check_vma=False,
    )
```

time: 450 us -> 87.8 us (0.20)
  waiting for transfers between devices: 340 us -> 0 us
  Pallas kernels: 0 us -> 78.9 us
  local copies, waits for them, and re-layouts: 59.4 us -> 8.53 us
  matrix products: 24.9 us -> 0 us
  between operations: 13.3 us -> 0.02 us
  other arithmetic: 10.9 us -> 0 us
    reduce_scatter x2 -> x0, waiting for transfers between devices: 213 us -> none  [the longest x1 115 us: shards(): lax.psum_scatter(partial_value, 'row', scatter_dimension=0, tiled=True)]
    all_gather x2 -> x0, waiting for transfers between devices: 127 us -> none  [the longest x1 64.1 us: shards(): left_cols = lax.all_gather(left_side, 'col', axis=1, tiled=True)]
    pallas_call x0 -> x1, Pallas kernels: none -> 78.9 us  [shards(): pl.pallas_call(kernel, out_shape=jax.ShapeDtypeStruct(arrays[0].shape, BF...]
    all_gather x2 -> x0, local copies, waits for them, and re-layouts: 30.9 us -> none  [the longest x1 23 us: shards(): right_rows = lax.all_gather(right_side, 'row', axis=0, tiled=True)]
    dot_general x10 -> x0, matrix products: 24.9 us -> none  [the longest x1 11.3 us: shards(): jnp.einsum('ikh,jkh->ijh', left_side, right_rows, preferred_element_type=...]
    transpose x2 -> x0, local copies, waits for them, and re-layouts: 21.9 us -> none  [the longest x1 11 us: shards(): jnp.einsum('ikh,jkh->ijh', left_side, right_rows, preferred_element_type=...]
    reduce_sum x7 -> x0, other arithmetic: 8.2 us -> none  [the longest x4 4.55 us: normalize(): variance = jnp.mean(centred * centred, axis=-1, keepdims=True)]
    unnamed x14 -> x21, local copies, waits for them, and re-layouts: 0.88 us -> 8.53 us
  transfers between devices with their start and end apart: 4 -> 0, of which waited for: 4 -> 0; matrix products, arithmetic and copies ran while one was open for 1% -> 0% of each run, Pallas kernels for 0% -> 0%
where the time goes in v1:
time: 87.8 us; the launch traced here: 87.4 us
  Pallas kernels  78.9 us (90%)
  local copies, waits for them, and re-layouts  8.53 us (10%)
    pallas_call x1, Pallas kernels, shards(): pl.pallas_call(kernel, out_shape=jax.ShapeDtypeStruct(arrays[0].shape, BF...  78.9 us
    unnamed x21, local copies, waits for them, and re-layouts  8.53 us

profile of v1, /device:TPU:1, one launch (start us, length us, event | category | flops | bytes accessed | tf_op | source)
XLA Modules:
  0.0 87.4 jit_solution(16639041441849120431)
XLA Ops:
  0.0 0.0 copy-start
  0.0 0.9 %copy-done = bf16[32,32,128]{2,1,0:T(8,128)(2,1)S(1)} copy-done((bf16[32,32,128]{2,1,0:T(8,128)(2,1)S(1)}, bf16[32,32,128]{2,1,0:T(8,128)(2,1)}, u32[]{:S(2)}) %copy-start) | copy-done | bytes 262168
  1.0 0.0 copy-start.1
  1.0 0.9 %copy-done.1 = bf16[2,128,256]{2,1,0:T(8,128)(2,1)S(1)} copy-done((bf16[2,128,256]{2,1,0:T(8,128)(2,1)S(1)}, bf16[2,128,256]{2,1,0:T(8,128)(2,1)}, u32[]{:S(2)}) %copy-start.1) | copy-done | bytes 131096
  1.9 0.0 copy-start.2
  1.9 0.9 %copy-done.2 = bf16[2,128,256]{2,1,0:T(8,128)(2,1)S(1)} copy-done((bf16[2,128,256]{2,1,0:T(8,128)(2,1)S(1)}, bf16[2,128,256]{2,1,0:T(8,128)(2,1)}, u32[]{:S(2)}) %copy-start.2) | copy-done | bytes 131096
  2.8 0.0 copy-start.3
  2.8 0.8 copy-done.3
  3.6 0.0 copy-start.4
  3.6 0.8 copy-done.4
  4.4 0.0 copy-start.5
  4.4 0.7 copy-done.5
  5.1 0.0 copy-start.6
  5.1 0.7 copy-done.6
  5.8 0.0 copy-start.7
  5.8 0.7 copy-done.7
  6.5 0.0 copy-start.8
  6.5 0.7 copy-done.8
  7.2 0.0 copy-start.9
  7.2 0.7 copy-done.9
  7.8 78.9 %shard_map.100 = bf16[32,32,128]{2,1,0:T(8,128)(2,1)S(1)} custom-call(bf16[32,32,128]{2,1,0:T(8,128)(2,1)S(1)} %copy-done, s32[512]{0:T(512)S(1)} %copy-done.5, f32[2,128]{1,0:T(2,128)S(1)} %copy-done.6, f32[2,128]{1,0:T(2,128)S(1)} %copy-done.7, bf16[2,128,256]{2,1,0:T(8,128)(2,1)S(1)} %copy-done.1, bf16[2,128,256]{2,1,0:T(8,128)(2,1)S(1)} %copy-done.2, ...), custom_call_target="tpu_custom_call" | custom-call | tf_op jit(solution)/shard_map/pallas_call | solution.py:242
  86.7 0.7 copy.12
Async XLA Ops:
  0.0 0.9 %copy-start = (bf16[32,32,128]{2,1,0:T(8,128)(2,1)S(1)}, bf16[32,32,128]{2,1,0:T(8,128)(2,1)}, u32[]{:S(2)}) copy-start(bf16[32,32,128]{2,1,0:T(8,128)(2,1)} %x_ref.1) | copy-start | bytes 786436
  1.0 0.9 %copy-start.1 = (bf16[2,128,256]{2,1,0:T(8,128)(2,1)S(1)}, bf16[2,128,256]{2,1,0:T(8,128)(2,1)}, u32[]{:S(2)}) copy-start(bf16[2,128,256]{2,1,0:T(8,128)(2,1)} %pw_ref.1) | copy-start | bytes 393220
  1.9 0.9 %copy-start.2 = (bf16[2,128,256]{2,1,0:T(8,128)(2,1)S(1)}, bf16[2,128,256]{2,1,0:T(8,128)(2,1)}, u32[]{:S(2)}) copy-start(bf16[2,128,256]{2,1,0:T(8,128)(2,1)} %gw_ref.1) | copy-start | bytes 393220
  2.8 0.8 copy-start.3
  3.6 0.8 copy-start.4
  4.4 0.7 copy-start.5
  5.1 0.7 copy-start.6
  5.8 0.7 copy-start.7
  6.5 0.7 copy-start.8
  7.2 0.7 copy-start.9

commit v2 on v1

v2 whole, which is shorter than its diff:
```python
import jax
import jax.numpy as jnp
from jax import lax
from jax.experimental import pallas as pl
from jax.experimental.pallas import tpu as pltpu
from jax.sharding import PartitionSpec as P

MESH = pl.DeviceIdType.MESH
F32 = jnp.float32
BF16 = jnp.bfloat16


def far_first(n):
    return n + 2 - (n // 2) * (2 * n - 1)


def dot(a, b, dims):
    return lax.dot_general(a, b, (dims, ((), ())), preferred_element_type=F32)


def sigmoid(v):
    return 0.5 * jnp.tanh(0.5 * v) + 0.5


def normalize(v, gain, bias):
    average = jnp.mean(v, axis=0, keepdims=True)
    centred = v - average
    variance = jnp.mean(centred * centred, axis=0, keepdims=True)
    return centred * lax.rsqrt(variance + 1e-05) * gain + bias


def chunk_swap(v):
    lane = lax.broadcasted_iota(jnp.int32, v[0].shape, 1)
    odd = (lane // 32) % 2 == 1
    high = lane >= 64

    def pair(a, b, shift, mask):
        return jnp.where(mask, pltpu.roll(b, shift, 1), a), jnp.where(
            mask, b, pltpu.roll(a, 128 - shift, 1)
        )

    a, b = pair(v[0], v[1], 32, odd)
    c, d = pair(v[2], v[3], 32, odd)
    a, c = pair(a, c, 64, high)
    b, d = pair(b, d, 64, high)
    return a, b, c, d


def kernel(
    x_hbm, mask_hbm, ng_hbm, nb_hbm, pw_hbm, gw_hbm, og_hbm, ob_hbm, fw_hbm, ow_hbm,
    out_ref,
    x_ref, mask_ref, ng_ref, nb_ref, pw_ref, gw_ref, og_ref, ob_ref, fw_ref, ow_ref,
    wt, ft, gb, zt, close, half, fsend, frecv, left, right, left_in, right_in, sums, bsend, brecv, wide,
    in_sem, entry, f_send, f_recv, b_send, b_recv, x_send, x_recv,
):
    row, col = lax.axis_index("row"), lax.axis_index("col")
    core = row % 2
    x, y, z = (row // 8) * 2 + col // 8, (row // 2) % 4, col % 8
    other = (row + 1 - 2 * core, col)

    hbm = (x_hbm, mask_hbm, ng_hbm, nb_hbm, pw_hbm, gw_hbm, og_hbm, ob_hbm, fw_hbm, ow_hbm)
    held = (x_ref, mask_ref, ng_ref, nb_ref, pw_ref, gw_ref, og_ref, ob_ref, fw_ref, ow_ref)
    inputs = [
        pltpu.make_async_copy(a, b, in_sem.at[k]) for k, (a, b) in enumerate(zip(hbm, held))
    ]
    for copy in inputs:
        copy.start()

    def line(x, y):
        x, y = (x + 4) % 4, (y + 4) % 4
        rr, base = (x // 2) * 4 + y, (x % 2) * 8
        return rr * 2 + core, base, rr * 16 + base

    chip = line(x, y)[2] + z
    ring = [(z + d) % 8 for d in range(8)]
    outward = (4, 3, 5, 2, 6, 1, 7, 0)

    barrier = pltpu.get_barrier_semaphore()
    for dx in (2, 1, 3):
        to_row, base, _ = line(x + dx, y)
        pl.semaphore_signal(barrier, inc=1, device_id=(to_row, base + z), device_id_type=MESH)
    for dy in (2, 1, 3, 0):
        to_row, base, _ = line(x, y + dy)
        for dz in outward[: 8 if dy else 7]:
            pl.semaphore_signal(
                barrier, inc=1, device_id=(to_row, base + ring[dz]), device_id_type=MESH
            )
    pl.semaphore_signal(barrier, inc=1, device_id=other, device_id_type=MESH)

    for copy in inputs:
        copy.wait()

    lane = lax.broadcasted_iota(jnp.int32, (8, 128), 1)
    first = lax.broadcasted_iota(jnp.int32, (8, 128), 0) + 8 * (lane // 32)
    row_mask = jnp.zeros((8, 128), jnp.int32)
    col_mask = jnp.zeros((8, 128), jnp.int32)
    for a in range(32):
        row_mask = jnp.where(first == a, mask_ref[row * 32 + a], row_mask)
        col_mask = jnp.where(lane % 32 == a, mask_ref[col * 32 + a], col_mask)
    token_mask = row_mask.astype(F32) * col_mask.astype(F32)

    def prepare(u):
        for k in range(2):
            wt[u, pl.ds(128 * k, 128)] = pw_ref[u, :, pl.ds(128 * k, 128)].T
            wt[u, pl.ds(256 + 128 * k, 128)] = gw_ref[u, :, pl.ds(128 * k, 128)].T
        wt[u, pl.ds(512, 128)] = ow_ref[u].T
        ft[u] = fw_ref[u].T
        for k, ref in enumerate((ng_ref, nb_ref, og_ref, ob_ref)):
            gb[4 * u + k] = jnp.broadcast_to(ref[pl.ds(u, 1), :], (128, 128)).T

    def project(u, s, z_s):
        normed = normalize(z_s, gb[4 * u], gb[4 * u + 1]).astype(BF16)
        product = dot(wt[u], normed, ((1,), (0,)))
        close[s] = sigmoid(product[512:])
        half[pl.ds(s, 256, stride=8), :] = (
            sigmoid(product[256:512]) * product[:256] * token_mask[s : s + 1]
        )

    def send_line(u, dx, dy, m):
        to_row, base, p = line(x + dx, y + dy)
        rows = pl.multiple_of(p * 8, 64)
        fsend[u, pl.ds(p, 8)] = jnp.concatenate(
            [
                half[pl.ds(rows, 64), :].reshape(8, 8, 128),
                half[pl.ds(rows + 1024, 64), :].reshape(8, 8, 128),
            ],
            axis=1,
        ).astype(BF16)
        for dz in outward:
            to = p + ring[dz]

            def send():
                pltpu.make_async_remote_copy(
                    fsend.at[u, to], frecv.at[u, chip], f_send.at[u], f_recv.at[u, m],
                    device_id=(to_row, base + ring[dz]), device_id_type=MESH,
                ).start()

            if dz:
                send()
            else:
                here = to == chip
                pl.when(jnp.logical_not(here))(send)

                @pl.when(here)
                def _():
                    pltpu.make_async_copy(
                        fsend.at[u, to], frecv.at[u, chip], f_recv.at[u, m]
                    ).start()

    def whole(src, dst, send, recv):
        return pltpu.make_async_remote_copy(
            src, dst, send, recv, device_id=other, device_id_type=MESH
        )

    def arrange_line(u, dx, dy, m):
        p = line(x - dx, y - dy)[2]
        part = pl.ds(p, 8)
        whole(fsend.at[u, part], frecv.at[u, part], f_send.at[u], f_recv.at[u, m]).wait_recv()
        rr, g = p // 16, (p // 8) % 2
        rows = pl.ds(pl.multiple_of(rr * 32, 32), 32)
        lanes = pl.ds(pl.multiple_of(g * 128, 128), 128)
        for t in range(2):
            swapped = chunk_swap([frecv[u, p + 2 * k + t].astype(F32) for k in range(4)])
            left[u, t, rows, lanes] = jnp.concatenate([v[:8] for v in swapped], axis=0).astype(BF16)
            right[u, t, rows, lanes] = jnp.concatenate([v[8:] for v in swapped], axis=0).astype(BF16)
        whole(
            right.at[u, :, rows, lanes], right_in.at[u, :, rows, lanes], x_send.at[u], x_recv.at[u]
        ).start()
        if u == 1:
            whole(
                left.at[u, 1 - core, rows, lanes], left_in.at[rows, lanes], x_send.at[2], x_recv.at[2]
            ).start()

    def send_sums(u, ts):
        ts = list(ts)

        @pl.loop(0, 16)
        def _(n):
            to_row, base, p = line(x + far_first(n // 4), y + far_first(n % 4))
            rr, g = p // 16, (p // 8) % 2
            lanes = pl.ds(pl.multiple_of(g * 128, 128), 128)
            for t in ts:
                tiles = [
                    sums[t, pl.ds(pl.multiple_of(rr * 32, 32) + 8 * k, 8), lanes] for k in range(4)
                ]
                for k, tile in enumerate(chunk_swap(tiles)):
                    bsend[u, p + 2 * k + t] = tile.astype(BF16)
            for t in ts:
                for d in (4, 2, 6, 0):
                    to_z = (z + d + (z + t) % 2) % 8
                    to = p + to_z

                    def send():
                        pltpu.make_async_remote_copy(
                            bsend.at[u, to], brecv.at[u, chip], b_send.at[u], b_recv.at[u],
                            device_id=(to_row, base + to_z), device_id_type=MESH,
                        ).start()

                    if d:
                        send()
                    else:
                        here = to == chip
                        pl.when(jnp.logical_not(here))(send)

                        @pl.when(here)
                        def _():
                            pltpu.make_async_copy(
                                bsend.at[u, to], brecv.at[u, chip], b_recv.at[u]
                            ).start()

    def receive_sums(u):
        whole(bsend.at[u], brecv.at[u], b_send.at[u], b_recv.at[u]).wait_recv()
        wide[...] = brecv[u].astype(F32).reshape(1024, 128)

    def finish(u, s):
        summed = wide[pl.ds(s, 128, stride=8), :]
        lifted = normalize(summed, gb[4 * u + 2], gb[4 * u + 3]).astype(BF16)
        update = close[s] * dot(ft[u], lifted, ((1,), (0,)))
        return (zt[s].astype(F32) + update).astype(BF16)

    prepare(0)
    for s in range(8):
        z_s = jnp.concatenate([x_ref[8 * k + s] for k in range(4)], axis=0).T
        zt[s] = z_s
        project(0, s, z_s.astype(F32))

    pl.semaphore_wait(barrier, 35)
    for dx in (2, 1, 3):
        to_row, base, _ = line(x + dx, y)
        pl.semaphore_signal(
            entry.at[dx], inc=1, device_id=(to_row, base + z), device_id_type=MESH
        )
    near_first = (0, 1, 3, 2)
    for k, dx in enumerate(near_first):
        if dx:
            pl.semaphore_wait(entry.at[4 - dx], 1)

        @pl.loop(0, 4)
        def _(n):
            send_line(0, dx, far_first(n), 4 * k + n)

    prepare(1)
    for k, dx in enumerate(near_first):

        @pl.loop(0, 4)
        def _(n):
            arrange_line(0, dx, far_first(n), 4 * k + n)

    swap = whole(right.at[0], right_in.at[0], x_send.at[0], x_recv.at[0])

    def outgoing(t, operand):
        sums[t] = dot(left[0, 0], operand[0], ((1,), (1,))) + dot(
            left[0, 1], operand[1], ((1,), (1,))
        )

    outgoing(core, right.at[0])
    send_sums(0, [core])
    swap.wait_recv()
    outgoing(1 - core, right_in.at[0])
    send_sums(0, [1 - core])
    receive_sums(0)

    for s in range(8):
        z_s = finish(0, s)
        zt[s] = z_s
        project(1, s, z_s.astype(F32))

    @pl.loop(0, 16)
    def _(n):
        send_line(1, far_first(n // 4), far_first(n % 4), n)

    @pl.loop(0, 16)
    def _(n):
        arrange_line(1, far_first(n // 4), far_first(n % 4), n)

    swap_left = whole(left.at[1, 1 - core], left_in, x_send.at[2], x_recv.at[2])
    swap_right = whole(right.at[1], right_in.at[1], x_send.at[1], x_recv.at[1])
    for t in range(2):
        sums[t] = dot(left[1, core], right[1, t], ((0,), (0,)))
    swap_left.wait_recv()
    swap_right.wait_recv()
    for t in range(2):
        sums[t] = sums[t] + dot(left_in[...], right_in[1, t], ((0,), (0,)))
    send_sums(1, [0, 1])
    receive_sums(1)

    for s in range(8):
        z_s = finish(1, s).T
        for k in range(4):
            out_ref[8 * k + s] = z_s[32 * k : 32 * k + 32]

    swap.wait_send()
    swap_left.wait_send()
    swap_right.wait_send()
    most = pl.ds(0, 127)
    for u in range(2):
        whole(fsend.at[u, most], frecv.at[u, most], f_send.at[u], f_recv.at[u, 0]).wait_send()
        whole(bsend.at[u, most], brecv.at[u, most], b_send.at[u], b_recv.at[u]).wait_send()


def shards(*arrays):
    vmem = pl.BlockSpec(memory_space=pltpu.VMEM)
    hbm = pl.BlockSpec(memory_space=pltpu.HBM)
    return pl.pallas_call(
        kernel,
        out_shape=jax.ShapeDtypeStruct(arrays[0].shape, BF16),
        in_specs=[hbm] * 10,
        out_specs=vmem,
        scratch_shapes=[
            (pltpu.SMEM if array.ndim == 1 else pltpu.VMEM)(array.shape, array.dtype)
            for array in arrays
        ]
        + [
            pltpu.VMEM((2, 640, 128), BF16),
            pltpu.VMEM((2, 128, 128), BF16),
            pltpu.VMEM((8, 128, 128), F32),
            pltpu.VMEM((8, 128, 128), BF16),
            pltpu.VMEM((8, 128, 128), F32),
            pltpu.VMEM((2048, 128), F32),
            pltpu.VMEM((2, 128, 16, 128), BF16),
            pltpu.VMEM((2, 128, 16, 128), BF16),
            pltpu.VMEM((2, 2, 256, 256), BF16),
            pltpu.VMEM((2, 2, 256, 256), BF16),
            pltpu.VMEM((256, 256), BF16),
            pltpu.VMEM((2, 2, 256, 256), BF16),
            pltpu.VMEM((2, 256, 256), F32),
            pltpu.VMEM((2, 128, 8, 128), BF16),
            pltpu.VMEM((2, 128, 8, 128), BF16),
            pltpu.VMEM((1024, 128), F32),
            pltpu.SemaphoreType.DMA((10,)),
            pltpu.SemaphoreType.REGULAR((4,)),
            pltpu.SemaphoreType.DMA((2,)),
            pltpu.SemaphoreType.DMA((2, 16)),
            pltpu.SemaphoreType.DMA((2,)),
            pltpu.SemaphoreType.DMA((2,)),
            pltpu.SemaphoreType.DMA((3,)),
            pltpu.SemaphoreType.DMA((3,)),
        ],
        compiler_params=pltpu.CompilerParams(
            collective_id=0, has_side_effects=True, vmem_limit_bytes=32 << 20
        ),
    )(*arrays)


def solution(mesh):
    return jax.shard_map(
        shards,
        mesh=mesh,
        in_specs=(P("row", "col", None), P(), P(), P(), P(), P(), P(), P(), P(), P()),
        out_specs=P("row", "col", None),
        check_vma=False,
    )
```

time: 87.8 us -> 75.8 us (0.86)
  Pallas kernels: 78.9 us -> 66.9 us
    pallas_call x1, Pallas kernels: 78.9 us -> 66.9 us  [shards(): pl.pallas_call(kernel, out_shape=jax.ShapeDtypeStruct(arrays[0].shape, BF...]
where the time goes in v2:
time: 75.8 us; the launch traced here: 75.5 us
  Pallas kernels  66.9 us (88%)
  local copies, waits for them, and re-layouts  8.53 us (11%)
    pallas_call x1, Pallas kernels, shards(): pl.pallas_call(kernel, out_shape=jax.ShapeDtypeStruct(arrays[0].shape, BF...  66.9 us
    unnamed x21, local copies, waits for them, and re-layouts  8.53 us

profile of v2, /device:TPU:1, one launch (start us, length us, event | category | flops | bytes accessed | tf_op | source)
XLA Modules:
  0.0 75.5 jit_solution(1513707139680320592)
XLA Ops:
  0.0 0.0 copy-start
  0.0 0.9 %copy-done = bf16[32,32,128]{2,1,0:T(8,128)(2,1)S(1)} copy-done((bf16[32,32,128]{2,1,0:T(8,128)(2,1)S(1)}, bf16[32,32,128]{2,1,0:T(8,128)(2,1)}, u32[]{:S(2)}) %copy-start) | copy-done | bytes 262168
  1.0 0.0 copy-start.1
  1.0 0.9 %copy-done.1 = bf16[2,128,256]{2,1,0:T(8,128)(2,1)S(1)} copy-done((bf16[2,128,256]{2,1,0:T(8,128)(2,1)S(1)}, bf16[2,128,256]{2,1,0:T(8,128)(2,1)}, u32[]{:S(2)}) %copy-start.1) | copy-done | bytes 131096
  1.9 0.0 copy-start.2
  1.9 0.9 %copy-done.2 = bf16[2,128,256]{2,1,0:T(8,128)(2,1)S(1)} copy-done((bf16[2,128,256]{2,1,0:T(8,128)(2,1)S(1)}, bf16[2,128,256]{2,1,0:T(8,128)(2,1)}, u32[]{:S(2)}) %copy-start.2) | copy-done | bytes 131096
  2.8 0.0 copy-start.3
  2.8 0.8 %copy-done.3 = bf16[2,128,128]{2,1,0:T(8,128)(2,1)S(1)} copy-done((bf16[2,128,128]{2,1,0:T(8,128)(2,1)S(1)}, bf16[2,128,128]{2,1,0:T(8,128)(2,1)}, u32[]{:S(2)}) %copy-start.3) | copy-done | bytes 65560
  3.6 0.0 copy-start.4
  3.6 0.8 %copy-done.4 = bf16[2,128,128]{2,1,0:T(8,128)(2,1)S(1)} copy-done((bf16[2,128,128]{2,1,0:T(8,128)(2,1)S(1)}, bf16[2,128,128]{2,1,0:T(8,128)(2,1)}, u32[]{:S(2)}) %copy-start.4) | copy-done | bytes 65560
  4.4 0.0 copy-start.5
  4.4 0.7 copy-done.5
  5.1 0.0 copy-start.6
  5.1 0.7 copy-done.6
  5.8 0.0 copy-start.7
  5.8 0.7 copy-done.7
  6.5 0.0 copy-start.8
  6.5 0.7 copy-done.8
  7.2 0.0 copy-start.9
  7.2 0.7 copy-done.9
  7.8 66.9 %shard_map.100 = bf16[32,32,128]{2,1,0:T(8,128)(2,1)S(1)} custom-call(bf16[32,32,128]{2,1,0:T(8,128)(2,1)S(1)} %copy-done, s32[512]{0:T(512)S(1)} %copy-done.5, f32[2,128]{1,0:T(2,128)S(1)} %copy-done.6, f32[2,128]{1,0:T(2,128)S(1)} %copy-done.7, bf16[2,128,256]{2,1,0:T(8,128)(2,1)S(1)} %copy-done.1, bf16[2,128,256]{2,1,0:T(8,128)(2,1)S(1)} %copy-done.2, ...), custom_call_target="tpu_custom_call" | custom-call | tf_op jit(solution)/shard_map/pallas_call | solution.py:304
  74.8 0.7 copy.12
Async XLA Ops:
  0.0 0.9 %copy-start = (bf16[32,32,128]{2,1,0:T(8,128)(2,1)S(1)}, bf16[32,32,128]{2,1,0:T(8,128)(2,1)}, u32[]{:S(2)}) copy-start(bf16[32,32,128]{2,1,0:T(8,128)(2,1)} %x_hbm.1) | copy-start | bytes 786436
  1.0 0.9 %copy-start.1 = (bf16[2,128,256]{2,1,0:T(8,128)(2,1)S(1)}, bf16[2,128,256]{2,1,0:T(8,128)(2,1)}, u32[]{:S(2)}) copy-start(bf16[2,128,256]{2,1,0:T(8,128)(2,1)} %pw_hbm.1) | copy-start | bytes 393220
  1.9 0.9 %copy-start.2 = (bf16[2,128,256]{2,1,0:T(8,128)(2,1)S(1)}, bf16[2,128,256]{2,1,0:T(8,128)(2,1)}, u32[]{:S(2)}) copy-start(bf16[2,128,256]{2,1,0:T(8,128)(2,1)} %gw_hbm.1) | copy-start | bytes 393220
  2.8 0.8 %copy-start.3 = (bf16[2,128,128]{2,1,0:T(8,128)(2,1)S(1)}, bf16[2,128,128]{2,1,0:T(8,128)(2,1)}, u32[]{:S(2)}) copy-start(bf16[2,128,128]{2,1,0:T(8,128)(2,1)} %fw_hbm.1) | copy-start | bytes 196612
  3.6 0.8 %copy-start.4 = (bf16[2,128,128]{2,1,0:T(8,128)(2,1)S(1)}, bf16[2,128,128]{2,1,0:T(8,128)(2,1)}, u32[]{:S(2)}) copy-start(bf16[2,128,128]{2,1,0:T(8,128)(2,1)} %ow_hbm.1) | copy-start | bytes 196612
  4.4 0.7 copy-start.5
  5.1 0.7 copy-start.6
  5.8 0.7 copy-start.7
  6.5 0.7 copy-start.8
  7.2 0.7 copy-start.9

commit v3 on v2

--- a/solution.py
+++ b/solution.py
@@ -230,21 +230,30 @@
         pl.semaphore_signal(
             entry.at[dx], inc=1, device_id=(to_row, base + z), device_id_type=MESH
         )
-    near_first = (0, 1, 3, 2)
-    for k, dx in enumerate(near_first):
-        if dx:
-            pl.semaphore_wait(entry.at[4 - dx], 1)
-
-        @pl.loop(0, 4)
-        def _(n):
-            send_line(0, dx, far_first(n), 4 * k + n)
+
+    def outer(n):
+        return far_first(n % 3), far_first((n // 3 + n % 3) % 4), 4 + n
+
+    @pl.loop(0, 4)
+    def _(n):
+        send_line(0, 0, far_first(n), n)
+
+    for dx in (2, 1, 3):
+        pl.semaphore_wait(entry.at[dx], 1)
+
+    @pl.loop(0, 12)
+    def _(n):
+        send_line(0, *outer(n))
 
     prepare(1)
-    for k, dx in enumerate(near_first):
-
-        @pl.loop(0, 4)
-        def _(n):
-            arrange_line(0, dx, far_first(n), 4 * k + n)
+
+    @pl.loop(0, 4)
+    def _(n):
+        arrange_line(0, 0, far_first(n), n)
+
+    @pl.loop(0, 12)
+    def _(n):
+        arrange_line(0, *outer(n))
 
     swap = whole(right.at[0], right_in.at[0], x_send.at[0], x_recv.at[0])
 
@@ -265,13 +274,16 @@
         zt[s] = z_s
         project(1, s, z_s.astype(F32))
 
+    def mixed(n):
+        return far_first(n % 4), far_first((n // 4 + n) % 4), n
+
     @pl.loop(0, 16)
     def _(n):
-        send_line(1, far_first(n // 4), far_first(n % 4), n)
+        send_line(1, *mixed(n))
 
     @pl.loop(0, 16)
     def _(n):
-        arrange_line(1, far_first(n // 4), far_first(n % 4), n)
+        arrange_line(1, *mixed(n))
 
     swap_left = whole(left.at[1, 1 - core], left_in, x_send.at[2], x_recv.at[2])
     swap_right = whole(right.at[1], right_in.at[1], x_send.at[1], x_recv.at[1])
@@ -339,7 +351,7 @@
         compiler_params=pltpu.CompilerParams(
             collective_id=0, has_side_effects=True, vmem_limit_bytes=32 << 20
         ),
-    )(*arrays)
+    )(*(pltpu.with_memory_space_constraint(array, pltpu.HBM) for array in arrays))
 
 
 def solution(mesh):

time: 75.8 us -> 68.2 us (0.90)
  local copies, waits for them, and re-layouts: 8.53 us -> 0.71 us
    unnamed x21 -> x1, local copies, waits for them, and re-layouts: 8.53 us -> 0.71 us
where the time goes in v3:
time: 68.2 us; the launch traced here: 68.1 us
  Pallas kernels  67.4 us (99%)
  local copies, waits for them, and re-layouts  0.71 us (1%)
    pallas_call x1, Pallas kernels, shards(): pl.pallas_call(kernel, out_shape=jax.ShapeDtypeStruct(arrays[0].shape, BF...  67.4 us

profile of v3, /device:TPU:1, one launch (start us, length us, event | category | flops | bytes accessed | tf_op | source)
XLA Modules:
  0.0 68.1 jit_solution(14214862706416351848)
XLA Ops:
  0.0 67.4 %shard_map.100 = bf16[32,32,128]{2,1,0:T(8,128)(2,1)S(1)} custom-call(bf16[32,32,128]{2,1,0:T(8,128)(2,1)} %x_hbm.1, s32[512]{0:T(512)} %mask_hbm.1, f32[2,128]{1,0:T(2,128)} %ng_hbm.1, f32[2,128]{1,0:T(2,128)} %nb_hbm.1, bf16[2,128,256]{2,1,0:T(8,128)(2,1)} %pw_hbm.1, bf16[2,128,256]{2,1,0:T(8,128)(2,1)} %gw_hbm.1, f32[2,128]{1,0:T(2,128)} %og_hbm.1, ...), custom_call_target="tpu_custom_call" | custom-call | tf_op jit(solution)/shard_map/pallas_call | solution.py:316
  67.4 0.7 %copy.12 = bf16[32,32,128]{2,1,0:T(8,128)(2,1)} copy(bf16[32,32,128]{2,1,0:T(8,128)(2,1)S(1)} %shard_map.100) | data formatting | bytes 524288

commit v4 on v3

--- a/solution.py
+++ b/solution.py
@@ -50,8 +50,8 @@
     x_hbm, mask_hbm, ng_hbm, nb_hbm, pw_hbm, gw_hbm, og_hbm, ob_hbm, fw_hbm, ow_hbm,
     out_ref,
     x_ref, mask_ref, ng_ref, nb_ref, pw_ref, gw_ref, og_ref, ob_ref, fw_ref, ow_ref,
-    wt, ft, gb, zt, close, half, fsend, frecv, left, right, left_in, right_in, sums, bsend, brecv, wide,
-    in_sem, entry, f_send, f_recv, b_send, b_recv, x_send, x_recv,
+    wt, ft, gb, zt, close, half, fsend, frecv, lrecv, lrecv_1, left, right, right_in, turned, sums, bsend, brecv, wide,
+    in_sem, entry, f_send, f_recv, l_send, l_recv, l_recv_1, b_send, b_recv, x_send, x_recv,
 ):
     row, col = lax.axis_index("row"), lax.axis_index("col")
     core = row % 2
@@ -116,97 +116,74 @@
             sigmoid(product[256:512]) * product[:256] * token_mask[s : s + 1]
         )
 
-    def send_line(u, dx, dy, m):
+    def pack(u, side, p):
+        rows = pl.multiple_of(p * 8, 64)
+        fsend[u, side, pl.ds(p, 8)] = (
+            half[pl.ds(rows + 1024 * side, 64), :].reshape(8, 8, 128).astype(BF16)
+        )
+
+    def send_tile(src, dst, send_sem, recv_sem, device, here):
+        def send():
+            pltpu.make_async_remote_copy(
+                src, dst, send_sem, recv_sem, device_id=device, device_id_type=MESH
+            ).start()
+
+        if here is False:
+            send()
+        else:
+            pl.when(jnp.logical_not(here))(send)
+
+            @pl.when(here)
+            def _():
+                pltpu.make_async_copy(src, dst, recv_sem).start()
+
+    def send_right(u, dx, dy, m):
         to_row, base, p = line(x + dx, y + dy)
-        rows = pl.multiple_of(p * 8, 64)
-        fsend[u, pl.ds(p, 8)] = jnp.concatenate(
-            [
-                half[pl.ds(rows, 64), :].reshape(8, 8, 128),
-                half[pl.ds(rows + 1024, 64), :].reshape(8, 8, 128),
-            ],
-            axis=1,
-        ).astype(BF16)
+        pack(u, 1, p)
         for dz in outward:
             to = p + ring[dz]
-
-            def send():
-                pltpu.make_async_remote_copy(
-                    fsend.at[u, to], frecv.at[u, chip], f_send.at[u], f_recv.at[u, m],
-                    device_id=(to_row, base + ring[dz]), device_id_type=MESH,
-                ).start()
-
-            if dz:
-                send()
-            else:
-                here = to == chip
-                pl.when(jnp.logical_not(here))(send)
-
-                @pl.when(here)
-                def _():
-                    pltpu.make_async_copy(
-                        fsend.at[u, to], frecv.at[u, chip], f_recv.at[u, m]
-                    ).start()
+            send_tile(
+                fsend.at[u, 1, to], frecv.at[u, chip], f_send.at[u], f_recv.at[u, m],
+                (to_row, base + ring[dz]), False if dz else to == chip,
+            )
 
     def whole(src, dst, send, recv):
         return pltpu.make_async_remote_copy(
             src, dst, send, recv, device_id=other, device_id_type=MESH
         )
 
-    def arrange_line(u, dx, dy, m):
+    def arrange(tiles):
+        return jnp.concatenate(chunk_swap([v.astype(F32) for v in tiles]), axis=0).astype(BF16)
+
+    def arrange_right(u, dx, dy, m):
         p = line(x - dx, y - dy)[2]
-        part = pl.ds(p, 8)
-        whole(fsend.at[u, part], frecv.at[u, part], f_send.at[u], f_recv.at[u, m]).wait_recv()
+        part = frecv.at[u, pl.ds(p, 8)]
+        whole(part, part, f_send.at[u], f_recv.at[u, m]).wait_recv()
         rr, g = p // 16, (p // 8) % 2
         rows = pl.ds(pl.multiple_of(rr * 32, 32), 32)
         lanes = pl.ds(pl.multiple_of(g * 128, 128), 128)
         for t in range(2):
-            swapped = chunk_swap([frecv[u, p + 2 * k + t].astype(F32) for k in range(4)])
-            left[u, t, rows, lanes] = jnp.concatenate([v[:8] for v in swapped], axis=0).astype(BF16)
-            right[u, t, rows, lanes] = jnp.concatenate([v[8:] for v in swapped], axis=0).astype(BF16)
+            right[u, t, rows, lanes] = arrange([frecv[u, p + 2 * k + t] for k in range(4)])
         whole(
             right.at[u, :, rows, lanes], right_in.at[u, :, rows, lanes], x_send.at[u], x_recv.at[u]
         ).start()
-        if u == 1:
-            whole(
-                left.at[u, 1 - core, rows, lanes], left_in.at[rows, lanes], x_send.at[2], x_recv.at[2]
-            ).start()
-
-    def send_sums(u, ts):
-        ts = list(ts)
-
-        @pl.loop(0, 16)
-        def _(n):
-            to_row, base, p = line(x + far_first(n // 4), y + far_first(n % 4))
-            rr, g = p // 16, (p // 8) % 2
-            lanes = pl.ds(pl.multiple_of(g * 128, 128), 128)
-            for t in ts:
+
+    def send_rows(u, rr, first_row, ts):
+        for t in ts:
+            for g in range(2):
                 tiles = [
-                    sums[t, pl.ds(pl.multiple_of(rr * 32, 32) + 8 * k, 8), lanes] for k in range(4)
+                    sums[t, pl.ds(first_row + 8 * k, 8), pl.ds(128 * g, 128)] for k in range(4)
                 ]
                 for k, tile in enumerate(chunk_swap(tiles)):
-                    bsend[u, p + 2 * k + t] = tile.astype(BF16)
-            for t in ts:
-                for d in (4, 2, 6, 0):
-                    to_z = (z + d + (z + t) % 2) % 8
-                    to = p + to_z
-
-                    def send():
-                        pltpu.make_async_remote_copy(
-                            bsend.at[u, to], brecv.at[u, chip], b_send.at[u], b_recv.at[u],
-                            device_id=(to_row, base + to_z), device_id_type=MESH,
-                        ).start()
-
-                    if d:
-                        send()
-                    else:
-                        here = to == chip
-                        pl.when(jnp.logical_not(here))(send)
-
-                        @pl.when(here)
-                        def _():
-                            pltpu.make_async_copy(
-                                bsend.at[u, to], brecv.at[u, chip], b_recv.at[u]
-                            ).start()
+                    bsend[u, rr * 16 + 8 * g + 2 * k + t] = tile.astype(BF16)
+        for d in (1, 0):
+            base = ((col // 8 + d) % 2) * 8
+            for dz in outward:
+                to = rr * 16 + base + ring[dz]
+                send_tile(
+                    bsend.at[u, to], brecv.at[u, chip], b_send.at[u], b_recv.at[u],
+                    (rr * 2 + core, base + ring[dz]), False if d or dz else to == chip,
+                )
 
     def receive_sums(u):
         whole(bsend.at[u], brecv.at[u], b_send.at[u], b_recv.at[u]).wait_recv()
@@ -236,37 +213,67 @@
 
     @pl.loop(0, 4)
     def _(n):
-        send_line(0, 0, far_first(n), n)
+        send_right(0, 0, far_first(n), n)
 
     for dx in (2, 1, 3):
         pl.semaphore_wait(entry.at[dx], 1)
 
     @pl.loop(0, 12)
     def _(n):
-        send_line(0, *outer(n))
+        send_right(0, *outer(n))
+
+    def part_of(n):
+        return (x // 2 + 1 - n // 4) % 2, far_first(n % 4)
+
+    @pl.loop(0, 8)
+    def _(n):
+        x_hi, dy = part_of(n)
+        for d in (1, 0):
+            to_row, base, p = line(2 * x_hi + (x + d) % 2, y + dy)
+            pack(0, 0, p)
+            for dz in outward:
+                to = p + ring[dz]
+                send_tile(
+                    fsend.at[0, 0, to], lrecv.at[chip], l_send.at[0], l_recv.at[n],
+                    (to_row, base + ring[dz]), False if d or dz else to == chip,
+                )
 
     prepare(1)
 
     @pl.loop(0, 4)
     def _(n):
-        arrange_line(0, 0, far_first(n), n)
+        arrange_right(0, 0, far_first(n), n)
 
     @pl.loop(0, 12)
     def _(n):
-        arrange_line(0, *outer(n))
+        arrange_right(0, *outer(n))
 
     swap = whole(right.at[0], right_in.at[0], x_send.at[0], x_recv.at[0])
-
-    def outgoing(t, operand):
-        sums[t] = dot(left[0, 0], operand[0], ((1,), (1,))) + dot(
-            left[0, 1], operand[1], ((1,), (1,))
-        )
-
-    outgoing(core, right.at[0])
-    send_sums(0, [core])
+    for t in range(2):
+        turned[core, t] = right[0, t].T
     swap.wait_recv()
-    outgoing(1 - core, right_in.at[0])
-    send_sums(0, [1 - core])
+    for t in range(2):
+        turned[1 - core, t] = right_in[0, t].T
+
+    @pl.loop(0, 8)
+    def _(n):
+        x_hi, dy = part_of(n)
+        rr = x_hi * 4 + (y + 4 - dy) % 4
+        part = lrecv.at[pl.ds(rr * 16, 16)]
+        whole(part, part, l_send.at[0], l_recv.at[n]).wait_recv()
+        rows = [
+            jnp.concatenate(
+                [arrange([lrecv[rr * 16 + 8 * g + 2 * k + t] for k in range(4)]) for g in range(2)],
+                axis=1,
+            )
+            for t in range(2)
+        ]
+        for t in range(2):
+            sums[t, pl.ds(0, 32)] = dot(rows[0], turned[t, 0], ((1,), (0,))) + dot(
+                rows[1], turned[t, 1], ((1,), (0,))
+            )
+        send_rows(0, rr, 0, range(2))
+
     receive_sums(0)
 
     for s in range(8):
@@ -279,21 +286,59 @@
 
     @pl.loop(0, 16)
     def _(n):
-        send_line(1, *mixed(n))
+        send_right(1, *mixed(n))
+
+    summing = z % 2
+
+    @pl.loop(0, 2)
+    def _(n):
+        x_hi = (x + 1 + n) % 2
+
+        @pl.loop(0, 8)
+        def _(k):
+            x_lo = (x + 1 + k // 4) % 2
+            to_row, base, p = line(2 * x_hi + x_lo, y + far_first(k % 4))
+            to_row = to_row - core + summing
+            pack(1, 0, p)
+            for dz in outward:
+                to = p + ring[dz]
+                here = jnp.logical_and(to == chip, summing == core)
+                send_tile(
+                    fsend.at[1, 0, to], lrecv_1.at[core, chip], l_send.at[1], l_recv_1.at[n],
+                    (to_row, base + ring[dz]), False if dz else here,
+                )
 
     @pl.loop(0, 16)
     def _(n):
-        arrange_line(1, *mixed(n))
-
-    swap_left = whole(left.at[1, 1 - core], left_in, x_send.at[2], x_recv.at[2])
-    swap_right = whole(right.at[1], right_in.at[1], x_send.at[1], x_recv.at[1])
-    for t in range(2):
-        sums[t] = dot(left[1, core], right[1, t], ((0,), (0,)))
-    swap_left.wait_recv()
-    swap_right.wait_recv()
-    for t in range(2):
-        sums[t] = sums[t] + dot(left_in[...], right_in[1, t], ((0,), (0,)))
-    send_sums(1, [0, 1])
+        arrange_right(1, *mixed(n))
+
+    swap_1 = whole(right.at[1], right_in.at[1], x_send.at[1], x_recv.at[1])
+    swap_1.wait_recv()
+
+    @pl.loop(0, 2)
+    def _(n):
+        g = (x // 2 + 1 - n) % 2
+        part = lrecv_1.at[0, pl.ds(0, 64)]
+        whole(part, part, l_send.at[1], l_recv_1.at[n]).wait_recv()
+
+        @pl.loop(0, 8)
+        def _(rr):
+            rows = pl.ds(pl.multiple_of(rr * 32, 32), 32)
+            for c in range(2):
+                left[c, rows, :] = arrange(
+                    [lrecv_1[c, rr * 16 + 8 * g + 2 * k + core] for k in range(4)]
+                )
+
+        for t in range(2):
+            sums[t] = dot(left[core], right[1, t], ((0,), (0,))) + dot(
+                left[1 - core], right_in[1, t], ((0,), (0,))
+            )
+
+        @pl.loop(0, 4)
+        def _(k):
+            to_y = (y + far_first(k)) % 4
+            send_rows(1, g * 4 + to_y, pl.multiple_of(to_y * 32, 32), range(2))
+
     receive_sums(1)
 
     for s in range(8):
@@ -302,12 +347,18 @@
             out_ref[8 * k + s] = z_s[32 * k : 32 * k + 32]
 
     swap.wait_send()
-    swap_left.wait_send()
-    swap_right.wait_send()
+    swap_1.wait_send()
     most = pl.ds(0, 127)
     for u in range(2):
-        whole(fsend.at[u, most], frecv.at[u, most], f_send.at[u], f_recv.at[u, 0]).wait_send()
+        for side, send in ((1, f_send), (0, l_send)):
+            sent = fsend.at[u, side, most]
+            whole(sent, sent, send.at[u], f_recv.at[u, 0]).wait_send()
         whole(bsend.at[u, most], brecv.at[u, most], b_send.at[u], b_recv.at[u]).wait_send()
+
+    @pl.when(summing != core)
+    def _():
+        sent = fsend.at[1, 0, 0]
+        whole(sent, sent, l_send.at[1], f_recv.at[1, 0]).wait_send()
 
 
 def shards(*arrays):
@@ -329,13 +380,15 @@
             pltpu.VMEM((8, 128, 128), BF16),
             pltpu.VMEM((8, 128, 128), F32),
             pltpu.VMEM((2048, 128), F32),
-            pltpu.VMEM((2, 128, 16, 128), BF16),
-            pltpu.VMEM((2, 128, 16, 128), BF16),
+            pltpu.VMEM((2, 2, 128, 8, 128), BF16),
+            pltpu.VMEM((2, 128, 8, 128), BF16),
+            pltpu.VMEM((128, 8, 128), BF16),
+            pltpu.VMEM((2, 128, 8, 128), BF16),
+            pltpu.VMEM((2, 256, 128), BF16),
             pltpu.VMEM((2, 2, 256, 256), BF16),
             pltpu.VMEM((2, 2, 256, 256), BF16),
-            pltpu.VMEM((256, 256), BF16),
             pltpu.VMEM((2, 2, 256, 256), BF16),
-            pltpu.VMEM((2, 256, 256), F32),
+            pltpu.VMEM((2, 128, 256), F32),
             pltpu.VMEM((2, 128, 8, 128), BF16),
             pltpu.VMEM((2, 128, 8, 128), BF16),
             pltpu.VMEM((1024, 128), F32),
@@ -344,9 +397,12 @@
             pltpu.SemaphoreType.DMA((2,)),
             pltpu.SemaphoreType.DMA((2, 16)),
             pltpu.SemaphoreType.DMA((2,)),
-            pltpu.SemaphoreType.DMA((2,)),
-            pltpu.SemaphoreType.DMA((3,)),
-            pltpu.SemaphoreType.DMA((3,)),
+            pltpu.SemaphoreType.DMA((8,)),
+            pltpu.SemaphoreType.DMA((2,)),
+            pltpu.SemaphoreType.DMA((2,)),
+            pltpu.SemaphoreType.DMA((2,)),
+            pltpu.SemaphoreType.DMA((2,)),
+            pltpu.SemaphoreType.DMA((2,)),
         ],
         compiler_params=pltpu.CompilerParams(
             collective_id=0, has_side_effects=True, vmem_limit_bytes=32 << 20

time: 68.2 us -> 63.7 us (0.934)
  Pallas kernels: 67.4 us -> 62.8 us
    pallas_call x1, Pallas kernels: 67.4 us -> 62.8 us  [shards(): pl.pallas_call(kernel, out_shape=jax.ShapeDtypeStruct(arrays[0].shape, BF...]
where the time goes in v4:
time: 63.7 us; the launch traced here: 63.6 us
  Pallas kernels  62.8 us (99%)
  local copies, waits for them, and re-layouts  0.71 us (1%)
    pallas_call x1, Pallas kernels, shards(): pl.pallas_call(kernel, out_shape=jax.ShapeDtypeStruct(arrays[0].shape, BF...  62.8 us

profile of v4, /device:TPU:1, one launch (start us, length us, event | category | flops | bytes accessed | tf_op | source)
XLA Modules:
  0.0 63.6 jit_solution(2746778641947784832)
XLA Ops:
  0.0 62.8 %shard_map.100 = bf16[32,32,128]{2,1,0:T(8,128)(2,1)S(1)} custom-call(bf16[32,32,128]{2,1,0:T(8,128)(2,1)} %x_hbm.1, s32[512]{0:T(512)} %mask_hbm.1, f32[2,128]{1,0:T(2,128)} %ng_hbm.1, f32[2,128]{1,0:T(2,128)} %nb_hbm.1, bf16[2,128,256]{2,1,0:T(8,128)(2,1)} %pw_hbm.1, bf16[2,128,256]{2,1,0:T(8,128)(2,1)} %gw_hbm.1, f32[2,128]{1,0:T(2,128)} %og_hbm.1, ...), custom_call_target="tpu_custom_call" | custom-call | tf_op jit(solution)/shard_map/pallas_call | solution.py:367
  62.9 0.7 %copy.12 = bf16[32,32,128]{2,1,0:T(8,128)(2,1)} copy(bf16[32,32,128]{2,1,0:T(8,128)(2,1)S(1)} %shard_map.100) | data formatting | bytes 524288

commit v5 on v4

--- a/solution.py
+++ b/solution.py
@@ -168,22 +168,24 @@
             right.at[u, :, rows, lanes], right_in.at[u, :, rows, lanes], x_send.at[u], x_recv.at[u]
         ).start()
 
-    def send_rows(u, rr, first_row, ts):
-        for t in ts:
-            for g in range(2):
-                tiles = [
-                    sums[t, pl.ds(first_row + 8 * k, 8), pl.ds(128 * g, 128)] for k in range(4)
-                ]
-                for k, tile in enumerate(chunk_swap(tiles)):
-                    bsend[u, rr * 16 + 8 * g + 2 * k + t] = tile.astype(BF16)
-        for d in (1, 0):
-            base = ((col // 8 + d) % 2) * 8
-            for dz in outward:
-                to = rr * 16 + base + ring[dz]
-                send_tile(
-                    bsend.at[u, to], brecv.at[u, chip], b_send.at[u], b_recv.at[u],
-                    (rr * 2 + core, base + ring[dz]), False if d or dz else to == chip,
-                )
+    def send_rows(u, parts):
+        for rr, first_row in parts:
+            for t in range(2):
+                for g in range(2):
+                    tiles = [
+                        sums[t, pl.ds(first_row + 8 * k, 8), pl.ds(128 * g, 128)] for k in range(4)
+                    ]
+                    for k, tile in enumerate(chunk_swap(tiles)):
+                        bsend[u, rr * 16 + 8 * g + 2 * k + t] = tile.astype(BF16)
+        for rr, _ in parts:
+            for d in (1, 0):
+                base = ((col // 8 + d) % 2) * 8
+                for dz in outward:
+                    to = rr * 16 + base + ring[dz]
+                    send_tile(
+                        bsend.at[u, to], brecv.at[u, chip], b_send.at[u], b_recv.at[u],
+                        (rr * 2 + core, base + ring[dz]), False if d or dz else to == chip,
+                    )
 
     def receive_sums(u):
         whole(bsend.at[u], brecv.at[u], b_send.at[u], b_recv.at[u]).wait_recv()
@@ -209,18 +211,18 @@
         )
 
     def outer(n):
-        return far_first(n % 3), far_first((n // 3 + n % 3) % 4), 4 + n
+        return (1 + 2 * (n // 4)) % 5 + 2 * (n // 8), far_first(n % 4), 4 + n
 
     @pl.loop(0, 4)
     def _(n):
         send_right(0, 0, far_first(n), n)
 
-    for dx in (2, 1, 3):
-        pl.semaphore_wait(entry.at[dx], 1)
-
-    @pl.loop(0, 12)
-    def _(n):
-        send_right(0, *outer(n))
+    for k, dx in enumerate((1, 3, 2)):
+        pl.semaphore_wait(entry.at[4 - dx], 1)
+
+        @pl.loop(0, 4)
+        def _(n):
+            send_right(0, dx, far_first(n), 4 + 4 * k + n)
 
     def part_of(n):
         return (x // 2 + 1 - n // 4) % 2, far_first(n % 4)
@@ -255,24 +257,27 @@
     for t in range(2):
         turned[1 - core, t] = right_in[0, t].T
 
-    @pl.loop(0, 8)
-    def _(n):
-        x_hi, dy = part_of(n)
-        rr = x_hi * 4 + (y + 4 - dy) % 4
-        part = lrecv.at[pl.ds(rr * 16, 16)]
-        whole(part, part, l_send.at[0], l_recv.at[n]).wait_recv()
-        rows = [
-            jnp.concatenate(
-                [arrange([lrecv[rr * 16 + 8 * g + 2 * k + t] for k in range(4)]) for g in range(2)],
-                axis=1,
-            )
-            for t in range(2)
-        ]
+    @pl.loop(0, 4)
+    def _(n):
+        parts, rows = [], ([], [])
+        for half_of in range(2):
+            x_hi, dy = part_of(2 * n + half_of)
+            rr = x_hi * 4 + (y + 4 - dy) % 4
+            part = lrecv.at[pl.ds(rr * 16, 16)]
+            whole(part, part, l_send.at[0], l_recv.at[2 * n + half_of]).wait_recv()
+            parts.append((rr, 32 * half_of))
+        for rr, _ in parts:
+            for t in range(2):
+                tiles = [
+                    arrange([lrecv[rr * 16 + 8 * g + 2 * k + t] for k in range(4)]) for g in range(2)
+                ]
+                rows[t].append(jnp.concatenate(tiles, axis=1))
+        rows = [jnp.concatenate(v, axis=0) for v in rows]
         for t in range(2):
-            sums[t, pl.ds(0, 32)] = dot(rows[0], turned[t, 0], ((1,), (0,))) + dot(
+            sums[t, pl.ds(0, 64)] = dot(rows[0], turned[t, 0], ((1,), (0,))) + dot(
                 rows[1], turned[t, 1], ((1,), (0,))
             )
-        send_rows(0, rr, 0, range(2))
+        send_rows(0, parts)
 
     receive_sums(0)
 
@@ -281,23 +286,23 @@
         zt[s] = z_s
         project(1, s, z_s.astype(F32))
 
-    def mixed(n):
-        return far_first(n % 4), far_first((n // 4 + n) % 4), n
+    def nth(n):
+        return far_first(n // 4), far_first(n % 4), n
 
     @pl.loop(0, 16)
     def _(n):
-        send_right(1, *mixed(n))
+        send_right(1, *nth(n))
 
     summing = z % 2
 
     @pl.loop(0, 2)
     def _(n):
-        x_hi = (x + 1 + n) % 2
+        x_lo = (x + 1 + n) % 2
 
         @pl.loop(0, 8)
         def _(k):
-            x_lo = (x + 1 + k // 4) % 2
-            to_row, base, p = line(2 * x_hi + x_lo, y + far_first(k % 4))
+            x_hi = (x // 2 + 1 + k % 2) % 2
+            to_row, base, p = line(2 * x_hi + x_lo, y + far_first(k // 2))
             to_row = to_row - core + summing
             pack(1, 0, p)
             for dz in outward:
@@ -310,34 +315,39 @@
 
     @pl.loop(0, 16)
     def _(n):
-        arrange_right(1, *mixed(n))
+        arrange_right(1, *nth(n))
 
     swap_1 = whole(right.at[1], right_in.at[1], x_send.at[1], x_recv.at[1])
     swap_1.wait_recv()
 
     @pl.loop(0, 2)
     def _(n):
-        g = (x // 2 + 1 - n) % 2
+        g = (x + 1 + n) % 2
         part = lrecv_1.at[0, pl.ds(0, 64)]
         whole(part, part, l_send.at[1], l_recv_1.at[n]).wait_recv()
 
-        @pl.loop(0, 8)
-        def _(rr):
-            rows = pl.ds(pl.multiple_of(rr * 32, 32), 32)
-            for c in range(2):
-                left[c, rows, :] = arrange(
-                    [lrecv_1[c, rr * 16 + 8 * g + 2 * k + core] for k in range(4)]
-                )
+        @pl.loop(0, 2)
+        def _(quarter):
+            for k in range(4):
+                rr = 4 * quarter + k
+                rows = pl.ds(pl.multiple_of(rr * 32, 32), 32)
+                for c in range(2):
+                    left[c, rows, :] = arrange(
+                        [lrecv_1[c, rr * 16 + 8 * g + 2 * m + core] for m in range(4)]
+                    )
 
         for t in range(2):
             sums[t] = dot(left[core], right[1, t], ((0,), (0,))) + dot(
                 left[1 - core], right_in[1, t], ((0,), (0,))
             )
 
-        @pl.loop(0, 4)
+        @pl.loop(0, 2)
         def _(k):
-            to_y = (y + far_first(k)) % 4
-            send_rows(1, g * 4 + to_y, pl.multiple_of(to_y * 32, 32), range(2))
+            parts = []
+            for m in range(2):
+                to_y = (y + far_first(2 * k + m)) % 4
+                parts.append((g * 4 + to_y, pl.multiple_of(to_y * 32, 32)))
+            send_rows(1, parts)
 
     receive_sums(1)
 

time: 63.7 us -> 62.7 us (0.984)
  Pallas kernels: 62.8 us -> 61.9 us
    pallas_call x1, Pallas kernels: 62.8 us -> 61.9 us  [shards(): pl.pallas_call(kernel, out_shape=jax.ShapeDtypeStruct(arrays[0].shape, BF...]
where the time goes in v5:
time: 62.7 us; the launch traced here: 62.6 us
  Pallas kernels  61.9 us (99%)
  local copies, waits for them, and re-layouts  0.71 us (1%)
    pallas_call x1, Pallas kernels, shards(): pl.pallas_call(kernel, out_shape=jax.ShapeDtypeStruct(arrays[0].shape, BF...  61.9 us

profile of v5, /device:TPU:1, one launch (start us, length us, event | category | flops | bytes accessed | tf_op | source)
XLA Modules:
  0.0 62.6 jit_solution(3723049730965509189)
XLA Ops:
  0.0 61.9 %shard_map.100 = bf16[32,32,128]{2,1,0:T(8,128)(2,1)S(1)} custom-call(bf16[32,32,128]{2,1,0:T(8,128)(2,1)} %x_hbm.1, s32[512]{0:T(512)} %mask_hbm.1, f32[2,128]{1,0:T(2,128)} %ng_hbm.1, f32[2,128]{1,0:T(2,128)} %nb_hbm.1, bf16[2,128,256]{2,1,0:T(8,128)(2,1)} %pw_hbm.1, bf16[2,128,256]{2,1,0:T(8,128)(2,1)} %gw_hbm.1, f32[2,128]{1,0:T(2,128)} %og_hbm.1, ...), custom_call_target="tpu_custom_call" | custom-call | tf_op jit(solution)/shard_map/pallas_call | solution.py:377
  61.9 0.7 %copy.12 = bf16[32,32,128]{2,1,0:T(8,128)(2,1)} copy(bf16[32,32,128]{2,1,0:T(8,128)(2,1)S(1)} %shard_map.100) | data formatting | bytes 524288

commit v6 on v5

--- a/solution.py
+++ b/solution.py
@@ -50,7 +50,7 @@
     x_hbm, mask_hbm, ng_hbm, nb_hbm, pw_hbm, gw_hbm, og_hbm, ob_hbm, fw_hbm, ow_hbm,
     out_ref,
     x_ref, mask_ref, ng_ref, nb_ref, pw_ref, gw_ref, og_ref, ob_ref, fw_ref, ow_ref,
-    wt, ft, gb, zt, close, half, fsend, frecv, lrecv, lrecv_1, left, right, right_in, turned, sums, bsend, brecv, wide,
+    wt, ft, gb, zt, normed, close, half, fsend, frecv, lrecv, lrecv_1, left, right, right_in, turned, sums, bsend, brecv, wide,
     in_sem, entry, f_send, f_recv, l_send, l_recv, l_recv_1, b_send, b_recv, x_send, x_recv,
 ):
     row, col = lax.axis_index("row"), lax.axis_index("col")
@@ -101,20 +101,28 @@
 
     def prepare(u):
         for k in range(2):
-            wt[u, pl.ds(128 * k, 128)] = pw_ref[u, :, pl.ds(128 * k, 128)].T
-            wt[u, pl.ds(256 + 128 * k, 128)] = gw_ref[u, :, pl.ds(128 * k, 128)].T
+            side = pl.ds(128 - 128 * k, 128)
+            wt[u, pl.ds(256 * k, 128)] = pw_ref[u, :, side].T
+            wt[u, pl.ds(256 * k + 128, 128)] = gw_ref[u, :, side].T
         wt[u, pl.ds(512, 128)] = ow_ref[u].T
         ft[u] = fw_ref[u].T
         for k, ref in enumerate((ng_ref, nb_ref, og_ref, ob_ref)):
             gb[4 * u + k] = jnp.broadcast_to(ref[pl.ds(u, 1), :], (128, 128)).T
 
-    def project(u, s, z_s):
-        normed = normalize(z_s, gb[4 * u], gb[4 * u + 1]).astype(BF16)
-        product = dot(wt[u], normed, ((1,), (0,)))
-        close[s] = sigmoid(product[512:])
-        half[pl.ds(s, 256, stride=8), :] = (
-            sigmoid(product[256:512]) * product[:256] * token_mask[s : s + 1]
+    def project_right(u, s, z_s):
+        normed[s] = normalize(z_s, gb[4 * u], gb[4 * u + 1]).astype(BF16)
+        product = dot(wt[u, pl.ds(0, 256)], normed[s], ((1,), (0,)))
+        half[pl.ds(1024 + s, 128, stride=8), :] = (
+            sigmoid(product[128:]) * product[:128] * token_mask[s : s + 1]
         )
+
+    def project_left(u):
+        for s in range(8):
+            product = dot(wt[u, pl.ds(256, 384)], normed[s], ((1,), (0,)))
+            half[pl.ds(s, 128, stride=8), :] = (
+                sigmoid(product[128:256]) * product[:128] * token_mask[s : s + 1]
+            )
+            close[s] = sigmoid(product[256:])
 
     def pack(u, side, p):
         rows = pl.multiple_of(p * 8, 64)
@@ -179,7 +187,7 @@
                         bsend[u, rr * 16 + 8 * g + 2 * k + t] = tile.astype(BF16)
         for rr, _ in parts:
             for d in (1, 0):
-                base = ((col // 8 + d) % 2) * 8
+                base = ((x + d + x // 2 + rr // 4) % 2) * 8
                 for dz in outward:
                     to = rr * 16 + base + ring[dz]
                     send_tile(
@@ -201,7 +209,7 @@
     for s in range(8):
         z_s = jnp.concatenate([x_ref[8 * k + s] for k in range(4)], axis=0).T
         zt[s] = z_s
-        project(0, s, z_s.astype(F32))
+        project_right(0, s, z_s.astype(F32))
 
     pl.semaphore_wait(barrier, 35)
     for dx in (2, 1, 3):
@@ -217,6 +225,7 @@
     def _(n):
         send_right(0, 0, far_first(n), n)
 
+    project_left(0)
     for k, dx in enumerate((1, 3, 2)):
         pl.semaphore_wait(entry.at[4 - dx], 1)
 
@@ -231,7 +240,7 @@
     def _(n):
         x_hi, dy = part_of(n)
         for d in (1, 0):
-            to_row, base, p = line(2 * x_hi + (x + d) % 2, y + dy)
+            to_row, base, p = line(2 * x_hi + (x + d + 1 - n // 4) % 2, y + dy)
             pack(0, 0, p)
             for dz in outward:
                 to = p + ring[dz]
@@ -284,7 +293,7 @@
     for s in range(8):
         z_s = finish(0, s)
         zt[s] = z_s
-        project(1, s, z_s.astype(F32))
+        project_right(1, s, z_s.astype(F32))
 
     def nth(n):
         return far_first(n // 4), far_first(n % 4), n
@@ -292,6 +301,8 @@
     @pl.loop(0, 16)
     def _(n):
         send_right(1, *nth(n))
+
+    project_left(1)
 
     summing = z % 2
 
@@ -388,6 +399,7 @@
             pltpu.VMEM((2, 128, 128), BF16),
             pltpu.VMEM((8, 128, 128), F32),
             pltpu.VMEM((8, 128, 128), BF16),
+            pltpu.VMEM((8, 128, 128), BF16),
             pltpu.VMEM((8, 128, 128), F32),
             pltpu.VMEM((2048, 128), F32),
             pltpu.VMEM((2, 2, 128, 8, 128), BF16),

time: 62.7 us -> 62.2 us (level)
  no operation moved by 1% of the time
where the time goes in v6:
time: 62.2 us; the launch traced here: 62.1 us
  Pallas kernels  61.4 us (99%)
  local copies, waits for them, and re-layouts  0.71 us (1%)
    pallas_call x1, Pallas kernels, shards(): pl.pallas_call(kernel, out_shape=jax.ShapeDtypeStruct(arrays[0].shape, BF...  61.4 us

profile of v6, /device:TPU:1, one launch (start us, length us, event | category | flops | bytes accessed | tf_op | source)
XLA Modules:
  0.0 62.1 jit_solution(15740450855530309773)
XLA Ops:
  0.0 61.4 %shard_map.100 = bf16[32,32,128]{2,1,0:T(8,128)(2,1)S(1)} custom-call(bf16[32,32,128]{2,1,0:T(8,128)(2,1)} %x_hbm.1, s32[512]{0:T(512)} %mask_hbm.1, f32[2,128]{1,0:T(2,128)} %ng_hbm.1, f32[2,128]{1,0:T(2,128)} %nb_hbm.1, bf16[2,128,256]{2,1,0:T(8,128)(2,1)} %pw_hbm.1, bf16[2,128,256]{2,1,0:T(8,128)(2,1)} %gw_hbm.1, f32[2,128]{1,0:T(2,128)} %og_hbm.1, ...), custom_call_target="tpu_custom_call" | custom-call | tf_op jit(solution)/shard_map/pallas_call | solution.py:388
  61.4 0.7 %copy.12 = bf16[32,32,128]{2,1,0:T(8,128)(2,1)} copy(bf16[32,32,128]{2,1,0:T(8,128)(2,1)S(1)} %shard_map.100) | data formatting | bytes 524288
